TPU v7x, 32 devices: a whole 2x2x4 slice. The times are simulated.
32 devices in a mesh: chan: 4 (over y, core), tile: 8 (over z, x).
Axes of the slice: x: 2, y: 2, z: 4, core: 2. Of those that a mesh axis runs over, the one named last changes fastest.
Arguments:
- intensity: bfloat16 [256, 256, 512], P('chan', 'tile'), may hold values from -12 to 12
- block_pick: int32 [8, 4, 4], P('tile', 'chan'), may hold values from 0 to 7, as said below
- owner_tile: int32 [8, 4, 4], P('tile', 'chan'), may hold values from 0 to 7, as said below
- source_index: int32 [8, 4, 4], P('tile', 'chan'), may hold values from 0 to 15
- mask_low: int32 [8, 4, 4, 1024], P('tile', 'chan'), may hold values from 0 to 63
- mask_high: int32 [8, 4, 4, 1024], P('tile', 'chan'), may hold values from 64 to 128
Outputs:
- moment_maps: float32 [8, 4, 8, 2, 1024], P('tile', 'chan')
- spectra: float32 [8, 4, 16, 256], P('tile', 'chan')
- smoothed: bfloat16 [256, 256, 512], P(None, 'tile', 'chan')
Inputs may be any that keep to these rules, and one draw needn't show every extreme that they name: `block_pick`: the 4 block numbers of one device are distinct. `owner_tile`: among the 4 sends of one device no owner appears more than 2 times; in every chan index some owner receives exactly 2 blocks from every device of that chan index.
All inputs are finite; a program needn't handle non-finite values.
Results may differ from a plain program's by a relative error of at most 0.0021.
Values may be sent and summed in bfloat16 or wider, within the bound.
A program may use at most 128 MiB of HBM per device.

v0:
```python
import jax
import jax.numpy as jnp
from jax import lax
from jax.sharding import PartitionSpec as P

BCH = 128
BPIX = 32
RADIUS = 2
CAP = 2
SRC_DEV = 16
SIGMA = 1.5


def with_halo(block, sides, width):
    for axis, dim in sides:
        count = lax.axis_size(axis)
        forward = [(i, i + 1) for i in range(count - 1)]
        backward = [(target, source) for source, target in forward]
        low = lax.ppermute(
            lax.slice_in_dim(block, block.shape[dim] - width, None, axis=dim), axis, forward
        )
        high = lax.ppermute(lax.slice_in_dim(block, 0, width, axis=dim), axis, backward)
        block = jnp.concatenate([low, block, high], axis=dim)
    return block


def gauss_weights():
    offsets = jnp.arange(-RADIUS, RADIUS + 1).astype(jnp.float32)
    raw_weights = jnp.exp(-offsets * offsets / (2.0 * SIGMA * SIGMA))
    return raw_weights / jnp.sum(raw_weights)


def smooth_tiles(framed):
    chan_total = framed.shape[0]
    rows_inner = framed.shape[1] - 2 * RADIUS
    cols_inner = framed.shape[2] - 2 * RADIUS
    chan_blocks = chan_total // BCH
    weights = gauss_weights()

    def smooth_block(block_index):
        first_chan = block_index * BCH
        middle = lax.dynamic_slice_in_dim(framed, first_chan, BCH, 0).astype(jnp.float32)
        before = lax.dynamic_slice_in_dim(framed, jnp.maximum(first_chan - 1, 0), 1, 0).astype(
            jnp.float32
        )
        before = before * (block_index > 0).astype(jnp.float32)
        after = lax.dynamic_slice_in_dim(
            framed, jnp.minimum(first_chan + BCH, chan_total - 1), 1, 0
        ).astype(jnp.float32)
        after = after * (block_index < chan_blocks - 1).astype(jnp.float32)
        lower = jnp.concatenate([before, middle[:-1]], axis=0)
        upper = jnp.concatenate([middle[1:], after], axis=0)
        hanning = 0.5 * middle + 0.25 * (lower + upper)
        row_pass = sum(
            (
                weights[offset] * hanning[:, offset : offset + rows_inner, :]
                for offset in range(2 * RADIUS + 1)
            )
        )
        col_pass = sum(
            (
                weights[offset] * row_pass[:, :, offset : offset + cols_inner]
                for offset in range(2 * RADIUS + 1)
            )
        )
        return col_pass.astype(jnp.bfloat16)

    stacked = lax.map(smooth_block, jnp.arange(chan_blocks, dtype=jnp.int32))
    return stacked.reshape(chan_total, rows_inner, cols_inner)


def per_device(intensity, block_pick, owner_tile, source_index, mask_low, mask_high):
    regrouped = lax.all_to_all(intensity, "chan", split_axis=2, concat_axis=0, tiled=True)
    framed = with_halo(regrouped, (("chan", 2), ("tile", 1)), RADIUS)
    tile_cube = smooth_tiles(framed)
    chan_total, rows_inner, cols_inner = tile_cube.shape
    chan_blocks = chan_total // BCH
    block_rows = rows_inner // BPIX
    block_cols = cols_inner // BPIX
    per_chan_block = block_rows * block_cols
    pixel_count = mask_low.shape[-1]
    picks = block_pick.reshape(-1)
    owners = owner_tile.reshape(-1)
    sources = source_index.reshape(-1)
    send_count = picks.shape[0]
    low_rows = mask_low.reshape(send_count, pixel_count)
    high_rows = mask_high.reshape(send_count, pixel_count)
    chan_of = picks // per_chan_block
    positions = jnp.arange(send_count, dtype=jnp.int32)
    earlier = (positions[None, :] < positions[:, None]) & (owners[None, :] == owners[:, None])
    ranking = jnp.sum(earlier.astype(jnp.int32), axis=1)
    slot_of = owners * CAP + ranking
    peer_count = lax.axis_size("tile")
    slot_total = peer_count * CAP
    filled = slot_of[None, :] == jnp.arange(slot_total, dtype=jnp.int32)[:, None]
    occupied = jnp.any(filled, axis=1)
    sender = jnp.sum(jnp.where(filled, positions[None, :], 0), axis=1)
    tags = jnp.stack([jnp.where(occupied, sources[sender], -1), chan_of[sender]], axis=1).reshape(
        peer_count, CAP, 2
    )
    block_total = chan_blocks * per_chan_block
    low_grid = jnp.zeros((block_total, pixel_count), jnp.int32).at[picks].set(low_rows)
    high_grid = jnp.zeros((block_total, pixel_count), jnp.int32).at[picks].set(high_rows)

    def to_tile(grid):
        shaped = grid.reshape(chan_blocks, block_rows, block_cols, BPIX, BPIX).transpose(
            0, 1, 3, 2, 4
        )
        return shaped.reshape(chan_blocks, 1, rows_inner, cols_inner)

    low_tile = to_tile(low_grid)
    high_tile = to_tile(high_grid)
    cube_blocks = tile_cube.reshape(chan_blocks, BCH, rows_inner, cols_inner)
    chan_pos = jnp.arange(BCH, dtype=jnp.int32).reshape(1, BCH, 1, 1)
    inside = (low_tile <= chan_pos) & (chan_pos < high_tile)
    masked = jnp.where(inside, cube_blocks.astype(jnp.float32), 0.0)
    maps_tile = jnp.sum(masked, axis=1)
    spectra_tile = jnp.sum(
        masked.reshape(chan_blocks, BCH, block_rows, BPIX, block_cols, BPIX), axis=(3, 5)
    )
    all_maps = (
        maps_tile.reshape(chan_blocks, block_rows, BPIX, block_cols, BPIX)
        .transpose(0, 1, 3, 2, 4)
        .reshape(block_total, pixel_count)
    )
    all_spectra = spectra_tile.transpose(0, 2, 3, 1).reshape(block_total, BCH)
    slot_picks = picks[sender]
    maps_slots = jnp.where(occupied[:, None], all_maps[slot_picks], 0.0).reshape(
        peer_count, CAP, pixel_count
    )
    spectra_slots = jnp.where(occupied[:, None], all_spectra[slot_picks], 0.0).reshape(
        peer_count, CAP, BCH
    )
    maps_here, spectra_here, tags_here = (
        lax.all_to_all(maps_slots, "tile", split_axis=0, concat_axis=0, tiled=True),
        lax.all_to_all(spectra_slots, "tile", split_axis=0, concat_axis=0, tiled=True),
        lax.all_to_all(tags, "tile", split_axis=0, concat_axis=0, tiled=True),
    )
    moment_maps = maps_here.reshape(1, 1, peer_count, CAP, pixel_count)
    keys_here = (tags_here[..., 0] * chan_blocks + tags_here[..., 1]).reshape(-1)
    selector = (
        keys_here[None, :] == jnp.arange(SRC_DEV * chan_blocks, dtype=jnp.int32)[:, None]
    ).astype(jnp.float32)
    spectra = jnp.dot(
        selector,
        spectra_here.reshape(-1, BCH),
        precision=lax.Precision.HIGHEST,
        preferred_element_type=jnp.float32,
    )
    return (moment_maps, spectra.reshape(1, 1, SRC_DEV, chan_blocks * BCH), tile_cube)


def solution(mesh):
    return jax.shard_map(
        per_device,
        mesh=mesh,
        in_specs=(
            P("chan", "tile", None),
            P("tile", "chan", None),
            P("tile", "chan", None),
            P("tile", "chan", None),
            P("tile", "chan", None, None),
            P("tile", "chan", None, None),
        ),
        out_specs=(
            P("tile", "chan", None, None, None),
            P("tile", "chan", None, None),
            P(None, "tile", "chan"),
        ),
        check_vma=False,
    )
```

profile of v0, /device:TPU:4, one launch (start us, length us, event | category | flops | bytes accessed | tf_op | source)
XLA Modules:
  0.0 183.7 jit_solution(6895373197032733767)
XLA Ops:
  0.6 8.8 %copy.87 = bf16[64,32,512]{0,1,2:T(8,128)(2,1)} copy(bf16[64,32,512]{2,1,0:T(8,128)(2,1)} %param.8) | data formatting | bytes 4194304 | tf_op args[0]
  9.4 5.9 %reshape.268 = bf16[4,2,131072]{2,1,0:T(2,128)(2,1)} reshape(bf16[512,32,64]{2,1,0:T(8,128)(2,1)} %bitcast.84) | data formatting | bytes 4194304
  15.3 3.7 %all-to-all-start = ((bf16[4,2,131072]{2,1,0:T(2,128)(2,1)}), bf16[4,2,131072]{2,1,0:T(2,128)(2,1)S(1)}, u32[]{:S(2)}, u32[]{:S(2)}) async-start(bf16[4,2,131072]{2,1,0:T(2,128)(2,1)} %reshape.268), calls=%async_computation | async-start | bytes 4194304 | tf_op jit(solution)/shard_map/all_to_all | solution.py:73
  19.4 0.7 gather_fusion
  20.1 0.7 gather_fusion.2
  22.3 20.5 %all-to-all-done = bf16[4,2,131072]{2,1,0:T(2,128)(2,1)S(1)} async-done(((bf16[4,2,131072]{2,1,0:T(2,128)(2,1)}), bf16[4,2,131072]{2,1,0:T(2,128)(2,1)S(1)}, u32[]{:S(2)}, u32[]{:S(2)}) %all-to-all-start) | async-done | bytes 2097184 | tf_op jit(solution)/shard_map/all_to_all | solution.py:73
  42.8 6.6 %all-to-all-start.2 = ((s32[8,2,2]{1,2,0:T(2,128)}), s32[8,2,2]{1,2,0:T(2,128)S(1)}, u32[]{:S(2)}, u32[]{:S(2)}) async-start(s32[8,2,2]{1,2,0:T(2,128)} %copy.98), calls=%async_computation.2 | async-start | bytes 16384 | tf_op jit(solution)/shard_map/all_to_all | solution.py:137
  49.4 4.0 %reshape.269 = bf16[512,32,64]{2,1,0:T(8,128)(2,1)} reshape(bf16[4,2,131072]{2,1,0:T(2,128)(2,1)S(1)} %all-to-all-done) | data formatting | bytes 4194304
  53.4 6.8 %copy.102 = bf16[64,32,4,128]{3,2,1,0:T(4,128)(2,1)} copy(bf16[64,32,4,128]{0,1,3,2:T(8,128)(2,1)} %bitcast.83) | data formatting | bytes 4194304 | tf_op jit(solution)/shard_map/all_to_all | solution.py:73
  60.2 1.9 %copy.89 = bf16[4,64,32,128]{3,2,1,0:T(8,128)(2,1)S(1)} copy(bf16[4,64,32,128]{3,0,2,1:T(4,128)(2,1)} %bitcast.85) | data formatting | bytes 4194304 | tf_op jit(solution)/shard_map/all_to_all | solution.py:73
  62.2 3.0 %fusion.34 = (bf16[256,32,2]{2,1,0:T(8,128)(2,1)}, bf16[256,32,2]{2,1,0:T(8,128)(2,1)}) fusion(bf16[256,32,128]{2,1,0:T(8,128)(2,1)S(1)} %bitcast.81), kind=kLoop, calls=%fused_computation.85 | loop fusion | bytes 131072 | tf_op jit(solution)/shard_map/slice | solution.py:20
  65.1 3.3 %copy.90 = bf16[256,32,2]{0,1,2:T(8,128)(2,1)S(1)} copy(bf16[256,32,2]{2,1,0:T(8,128)(2,1)} %get-tuple-element.92) | data formatting | bytes 65536 | tf_op jit(solution)/shard_map/slice | solution.py:20
  68.4 1.9 %collective-permute-start = (bf16[256,32,2]{0,1,2:T(8,128)(2,1)S(1)}, bf16[256,32,2]{0,1,2:T(8,128)(2,1)S(1)}, u32[]{:S(2)}, u32[]{:S(2)}) collective-permute-start(bf16[256,32,2]{0,1,2:T(8,128)(2,1)S(1)} %copy.90), channel_id=1, source_target_pairs={{0,8},{8,16},{16,24},{1,9},{9,17},{17,25},{2,10},{10,18},{18,26},{... | collective-permute-start | bytes 98312 | tf_op jit(solution)/shard_map/ppermute | solution.py:19
  70.3 3.3 %copy.91 = bf16[256,32,2]{0,1,2:T(8,128)(2,1)S(1)} copy(bf16[256,32,2]{2,1,0:T(8,128)(2,1)} %get-tuple-element.93) | data formatting | bytes 65536 | tf_op jit(solution)/shard_map/slice | solution.py:22
  73.6 3.8 %collective-permute-start.1 = (bf16[256,32,2]{0,1,2:T(8,128)(2,1)S(1)}, bf16[256,32,2]{0,1,2:T(8,128)(2,1)S(1)}, u32[]{:S(2)}, u32[]{:S(2)}) collective-permute-start(bf16[256,32,2]{0,1,2:T(8,128)(2,1)S(1)} %copy.91), channel_id=1, source_target_pairs={{8,0},{16,8},{24,16},{9,1},{17,9},{25,17},{10,2},{18,10},{26,18},{... | collective-permute-start | bytes 98312 | tf_op jit(solution)/shard_map/ppermute | solution.py:22
  78.0 4.2 %copy.92 = bf16[256,32,2]{2,1,0:T(8,128)(2,1)} copy(bf16[256,32,2]{0,1,2:T(8,128)(2,1)S(1)} %collective-permute-done) | data formatting | bytes 65536 | tf_op jit(solution)/shard_map/ppermute | solution.py:19
  82.3 4.2 %copy.93 = bf16[256,32,2]{2,1,0:T(8,128)(2,1)} copy(bf16[256,32,2]{0,1,2:T(8,128)(2,1)S(1)} %collective-permute-done.1) | data formatting | bytes 65536 | tf_op jit(solution)/shard_map/ppermute | solution.py:22
  86.5 4.3 %pad_maximum_fusion = bf16[256,32,132]{2,1,0:T(8,128)(2,1)S(1)} fusion(bf16[256,32,2]{2,1,0:T(8,128)(2,1)} %copy.93, bf16[256,32,128]{2,1,0:T(8,128)(2,1)S(1)} %bitcast.82, bf16[256,32,2]{2,1,0:T(8,128)(2,1)} %copy.92), kind=kLoop, calls=%fused_computation.33 | loop fusion | flops 6488064 | bytes 4325376 | tf_op jit(solution)/shard_map/concatenate | solution.py:23
  90.7 1.9 %copy-done.5 = bf16[256,32,132]{2,1,0:T(8,128)(2,1)} copy-done((bf16[256,32,132]{2,1,0:T(8,128)(2,1)}, bf16[256,32,132]{2,1,0:T(8,128)(2,1)S(1)}, u32[]{:S(2)}) %copy-start.5) | copy-done | bytes 2162712
  93.1 3.9 %collective-permute-start.2 = (bf16[256,2,132]{2,1,0:T(2,128)(2,1)S(1)}, bf16[256,2,132]{2,1,0:T(2,128)(2,1)S(1)}, u32[]{:S(2)}, u32[]{:S(2)}) collective-permute-start(bf16[256,2,132]{2,1,0:T(2,128)(2,1)S(1)} %get-tuple-element.90), channel_id=1, source_target_pairs={{0,1},{1,2},{2,3},{3,4},{4,5},{5,6},{6,7},{8,9},{9,10},{10,11},{11... | collective-permute-start | bytes 405512 | tf_op jit(solution)/shard_map/ppermute | solution.py:19
  97.0 1.3 collective-permute-start.3
  100.0 0.9 scatter_custom_fusion.1
  101.3 7.6 %copy.95 = bf16[256,32,132]{0,2,1:T(8,128)(2,1)} copy(bf16[256,32,132]{2,1,0:T(8,128)(2,1)} %copy-done.5) | data formatting | bytes 4325376 | tf_op jit(solution)/shard_map/concatenate | solution.py:23
  109.2 2.0 %pad_maximum_fusion.1 = bf16[256,36,132]{0,2,1:T(8,128)(2,1)S(1)} fusion(bf16[256,2,132]{0,2,1:T(8,128)(2,1)S(1)} %copy.96, bf16[256,32,132]{0,2,1:T(8,128)(2,1)} %copy.95, bf16[256,2,132]{0,2,1:T(8,128)(2,1)S(1)} %copy.94), kind=kLoop, calls=%fused_computation.40 | loop fusion | flops 2433024 | bytes 4866048 | tf_op jit(solution)/shard_map/concatenate | solution.py:23
  111.2 38.9 %while.12 = (s32[]{:T(128)}, bf16[2,128,32,128]{1,3,2,0:T(8,128)(2,1)}, f32[5]{0:T(128)S(1)}, s32[2]{0:T(128)S(1)}, bf16[256,36,132]{0,2,1:T(8,128)(2,1)S(1)}, /...) while((s32[]{:T(128)}, ...), condition=%wide.region_6.7_spmd, body=%wide.region_5.6_spmd.sunk | while | flops 14994001 | bytes 46544248 | solution.py:68
  113.8 3.0 %convert_multiply_fusion.3 = (f32[1,36,132]{0,2,1:T(8,128)}, f32[1,36,132]{0,2,1:T(8,128)}) fusion(f32[]{:T(128)} %bitcast.72, bf16[256,36,132]{0,2,1:T(8,128)(2,1)S(1)} %get-tuple-element.175, s32[]{:T(128)S(6)} %select_n.117, f32[]{:T(128)} %bitcast.73, s32[]{:T(128)S(6)} %max.7), kind=kLoop, calls=%fused_computation.10.clone.1 | loop fusion | flops 19008 | bytes 57040 | tf_op jit(solution)/shard_map/while/body/eval_jaxpr/mul | solution.py:50
  117.0 0.8 fusion.40
  117.8 0.9 copy-done.3
  118.7 0.8 copy-done.4
  119.4 1.4 fusion.41
  120.8 0.7 fusion.42
  121.4 3.8 %fusion.43 = f32[128,32,132]{0,2,1:T(8,128)S(1)} fusion(f32[128,36,132]{0,2,1:T(8,128)S(1)} %fusion.41, f32[]{:T(128)} %bitcast.74, f32[]{:T(128)} %bitcast.75, f32[]{:T(128)} %bitcast.76, f32[]{:T(128)} %bitcast.77, f32[]{:T(128)} %bitcast.78), kind=kLoop, calls=%fused_computation.13.clone.1 | loop fusion | flops 4866048 | bytes 12976148 | tf_op jit(solution)/shard_map/while/body/eval_jaxpr/add | solution.py:54
  125.3 5.4 %bitcast_dynamic-update-slice_fusion.2 = bf16[2,128,32,128]{1,3,2,0:T(8,128)(2,1)} fusion(bf16[2,128,32,128]{1,3,2,0:T(8,128)(2,1)} %get-tuple-element.158, s32[]{:T(128)} %get-tuple-element.157, f32[128,32,132]{0,2,1:T(8,128)S(1)} %fusion.43, f32[]{:T(128)} %bitcast.74, f32[]{:T(128)} %bitcast.75, f32[]{:T(128)} %bitcast.76, f32[]{:T(128)} %bitcast.77, ...), kind=kLoop, calls=%fused_computation.32.clone.1 | loop fusion | flops 5242880 | bytes 11537408 | tf_op jit(solution)/shard_map/while/body/jit(dynamic_update_index_in_dim)/dynamic_update_slice | solution.py:68
  133.2 3.0 %convert_multiply_fusion.3 = (f32[1,36,132]{0,2,1:T(8,128)}, f32[1,36,132]{0,2,1:T(8,128)}) fusion(f32[]{:T(128)} %bitcast.72, bf16[256,36,132]{0,2,1:T(8,128)(2,1)S(1)} %get-tuple-element.175, s32[]{:T(128)S(6)} %select_n.117, f32[]{:T(128)} %bitcast.73, s32[]{:T(128)S(6)} %max.7), kind=kLoop, calls=%fused_computation.10.clone.1 | loop fusion | flops 19008 | bytes 57040 | tf_op jit(solution)/shard_map/while/body/eval_jaxpr/mul | solution.py:50
  136.4 0.8 fusion.40
  137.2 0.9 copy-done.3
  138.1 0.8 copy-done.4
  138.8 1.4 fusion.41
  140.2 0.7 fusion.42
  140.9 3.8 %fusion.43 = f32[128,32,132]{0,2,1:T(8,128)S(1)} fusion(f32[128,36,132]{0,2,1:T(8,128)S(1)} %fusion.41, f32[]{:T(128)} %bitcast.74, f32[]{:T(128)} %bitcast.75, f32[]{:T(128)} %bitcast.76, f32[]{:T(128)} %bitcast.77, f32[]{:T(128)} %bitcast.78), kind=kLoop, calls=%fused_computation.13.clone.1 | loop fusion | flops 4866048 | bytes 12976148 | tf_op jit(solution)/shard_map/while/body/eval_jaxpr/add | solution.py:54
  144.7 5.4 %bitcast_dynamic-update-slice_fusion.2 = bf16[2,128,32,128]{1,3,2,0:T(8,128)(2,1)} fusion(bf16[2,128,32,128]{1,3,2,0:T(8,128)(2,1)} %get-tuple-element.158, s32[]{:T(128)} %get-tuple-element.157, f32[128,32,132]{0,2,1:T(8,128)S(1)} %fusion.43, f32[]{:T(128)} %bitcast.74, f32[]{:T(128)} %bitcast.75, f32[]{:T(128)} %bitcast.76, f32[]{:T(128)} %bitcast.77, ...), kind=kLoop, calls=%fused_computation.32.clone.1 | loop fusion | flops 5242880 | bytes 11537408 | tf_op jit(solution)/shard_map/while/body/jit(dynamic_update_index_in_dim)/dynamic_update_slice | solution.py:68
  150.1 6.1 %fusion.11 = (f32[2,128,128]{1,2,0:T(8,128)S(1)}, f32[2,32,128]{2,1,0:T(8,128)S(1)}) fusion(bf16[2,128,32,128]{1,3,2,0:T(8,128)(2,1)} %get-tuple-element.68, s32[2,32,128]{2,1,0:T(8,128)S(1)} %lt.89, s32[2,32,128]{2,1,0:T(8,128)S(1)} %le.17), kind=kLoop, calls=%fused_computation.35 | loop fusion | flops 7299072 | bytes 2326528 | tf_op jit(solution)/shard_map/reduce_sum | solution.py:118
  156.8 0.7 broadcast_select_fusion.1
  157.5 6.6 %all-to-all-start.3 = ((f32[8,2,128]{2,1,0:T(2,128)}), f32[8,2,128]{2,1,0:T(2,128)S(1)}, u32[]{:S(2)}, u32[]{:S(2)}) async-start(f32[8,2,128]{2,1,0:T(2,128)} %broadcast_select_fusion.1), calls=%async_computation.3 | async-start | bytes 16384 | tf_op jit(solution)/shard_map/all_to_all | solution.py:136
  165.0 0.7 broadcast_select_fusion
  165.7 4.5 %copy.101 = bf16[2,128,32,128]{3,2,1,0:T(8,128)(2,1)} copy(bf16[2,128,32,128]{1,3,2,0:T(8,128)(2,1)} %get-tuple-element.68) | data formatting | bytes 4194304 | tf_op jit(solution)/shard_map/while | solution.py:68
  170.6 5.6 %all-to-all-start.1 = ((f32[8,2,1024]{2,1,0:T(2,128)}), f32[8,2,1024]{2,1,0:T(2,128)S(1)}, u32[]{:S(2)}, u32[]{:S(2)}) async-start(f32[8,2,1024]{2,1,0:T(2,128)} %broadcast_select_fusion), calls=%async_computation.1 | async-start | bytes 131072 | tf_op jit(solution)/shard_map/all_to_all | solution.py:135
  176.9 6.2 %all-to-all-done.1 = f32[8,2,1024]{2,1,0:T(2,128)S(1)} async-done(((f32[8,2,1024]{2,1,0:T(2,128)}), f32[8,2,1024]{2,1,0:T(2,128)S(1)}, u32[]{:S(2)}, u32[]{:S(2)}) %all-to-all-start.1) | async-done | bytes 65568 | tf_op jit(solution)/shard_map/all_to_all | solution.py:135
  (68 shorter events, 10.1 us)
Async XLA Ops:
  0.6 98.4 %copy-start = (s32[1,1,4,1024]{3,2,1,0:T(4,128)S(1)}, s32[1,1,4,1024]{3,2,1,0:T(4,128)}, u32[]{:S(2)}) copy-start(s32[1,1,4,1024]{3,2,1,0:T(4,128)} %param.12) | copy-start | bytes 49156
  15.3 3.8 %copy-start.7 = (s32[1,1,4]{2,1,0:T(1,128)S(1)}, s32[1,1,4]{2,1,0:T(1,128)}, u32[]{:S(2)}) copy-start(s32[1,1,4]{2,1,0:T(1,128)} %param.10) | copy-start | bytes 52
  15.3 4.1 %copy-start.2 = (s32[1,1,4]{2,1,0:T(1,128)S(1)}, s32[1,1,4]{2,1,0:T(1,128)}, u32[]{:S(2)}) copy-start(s32[1,1,4]{2,1,0:T(1,128)} %param.9) | copy-start | bytes 52
  15.3 4.7 %copy-start.1 = (s32[1,1,4]{2,1,0:T(1,128)S(1)}, s32[1,1,4]{2,1,0:T(1,128)}, u32[]{:S(2)}) copy-start(s32[1,1,4]{2,1,0:T(1,128)} %param.11) | copy-start | bytes 52
  15.3 27.5 %all-to-all-start = ((bf16[4,2,131072]{2,1,0:T(2,128)(2,1)}), bf16[4,2,131072]{2,1,0:T(2,128)(2,1)S(1)}, u32[]{:S(2)}, u32[]{:S(2)}) async-start(bf16[4,2,131072]{2,1,0:T(2,128)(2,1)} %reshape.268), calls=%async_computation | async-start | bytes 4194304 | tf_op jit(solution)/shard_map/all_to_all | solution.py:73
  42.8 58.4 %all-to-all-start.2 = ((s32[8,2,2]{1,2,0:T(2,128)}), s32[8,2,2]{1,2,0:T(2,128)S(1)}, u32[]{:S(2)}, u32[]{:S(2)}) async-start(s32[8,2,2]{1,2,0:T(2,128)} %copy.98), calls=%async_computation.2 | async-start | bytes 16384 | tf_op jit(solution)/shard_map/all_to_all | solution.py:137
  68.4 9.7 %collective-permute-start = (bf16[256,32,2]{0,1,2:T(8,128)(2,1)S(1)}, bf16[256,32,2]{0,1,2:T(8,128)(2,1)S(1)}, u32[]{:S(2)}, u32[]{:S(2)}) collective-permute-start(bf16[256,32,2]{0,1,2:T(8,128)(2,1)S(1)} %copy.90), channel_id=1, source_target_pairs={{0,8},{8,16},{16,24},{1,9},{9,17},{17,25},{2,10},{10,18},{18,26},{... | collective-permute-start | bytes 98312 | tf_op jit(solution)/shard_map/ppermute | solution.py:19
  73.6 8.7 %collective-permute-start.1 = (bf16[256,32,2]{0,1,2:T(8,128)(2,1)S(1)}, bf16[256,32,2]{0,1,2:T(8,128)(2,1)S(1)}, u32[]{:S(2)}, u32[]{:S(2)}) collective-permute-start(bf16[256,32,2]{0,1,2:T(8,128)(2,1)S(1)} %copy.91), channel_id=1, source_target_pairs={{8,0},{16,8},{24,16},{9,1},{17,9},{25,17},{10,2},{18,10},{26,18},{... | collective-permute-start | bytes 98312 | tf_op jit(solution)/shard_map/ppermute | solution.py:22
  86.5 13.6 %copy-start.6 = (s32[1,1,4,1024]{3,2,1,0:T(4,128)S(1)}, s32[1,1,4,1024]{3,2,1,0:T(4,128)}, u32[]{:S(2)}) copy-start(s32[1,1,4,1024]{3,2,1,0:T(4,128)} %param.13) | copy-start | bytes 49156
  90.7 1.9 %copy-start.5 = (bf16[256,32,132]{2,1,0:T(8,128)(2,1)}, bf16[256,32,132]{2,1,0:T(8,128)(2,1)S(1)}, u32[]{:S(2)}) copy-start(bf16[256,32,132]{2,1,0:T(8,128)(2,1)S(1)} %pad_maximum_fusion) | copy-start | bytes 6488068
  93.1 15.8 %collective-permute-start.2 = (bf16[256,2,132]{2,1,0:T(2,128)(2,1)S(1)}, bf16[256,2,132]{2,1,0:T(2,128)(2,1)S(1)}, u32[]{:S(2)}, u32[]{:S(2)}) collective-permute-start(bf16[256,2,132]{2,1,0:T(2,128)(2,1)S(1)} %get-tuple-element.90), channel_id=1, source_target_pairs={{0,1},{1,2},{2,3},{3,4},{4,5},{5,6},{6,7},{8,9},{9,10},{10,11},{11... | collective-permute-start | bytes 405512 | tf_op jit(solution)/shard_map/ppermute | solution.py:19
  97.0 12.1 %collective-permute-start.3 = (bf16[256,2,132]{2,1,0:T(2,128)(2,1)S(1)}, bf16[256,2,132]{2,1,0:T(2,128)(2,1)S(1)}, u32[]{:S(2)}, u32[]{:S(2)}) collective-permute-start(bf16[256,2,132]{2,1,0:T(2,128)(2,1)S(1)} %get-tuple-element.91), channel_id=1, source_target_pairs={{1,0},{2,1},{3,2},{4,3},{5,4},{6,5},{7,6},{9,8},{10,9},{11,10},{12... | collective-permute-start | bytes 405512 | tf_op jit(solution)/shard_map/ppermute | solution.py:22
  116.9 1.7 copy-start.3
  117.0 2.5 %copy-start.4 = (f32[1,36,132]{0,2,1:T(8,128)S(1)}, f32[1,36,132]{0,2,1:T(8,128)}, u32[]{:S(2)}) copy-start(f32[1,36,132]{0,2,1:T(8,128)} %get-tuple-element.135) | copy-start | bytes 57028 | tf_op jit(solution)/shard_map/while
  136.4 1.7 copy-start.3
  136.4 2.5 %copy-start.4 = (f32[1,36,132]{0,2,1:T(8,128)S(1)}, f32[1,36,132]{0,2,1:T(8,128)}, u32[]{:S(2)}) copy-start(f32[1,36,132]{0,2,1:T(8,128)} %get-tuple-element.135) | copy-start | bytes 57028 | tf_op jit(solution)/shard_map/while
  157.5 13.1 %all-to-all-start.3 = ((f32[8,2,128]{2,1,0:T(2,128)}), f32[8,2,128]{2,1,0:T(2,128)S(1)}, u32[]{:S(2)}, u32[]{:S(2)}) async-start(f32[8,2,128]{2,1,0:T(2,128)} %broadcast_select_fusion.1), calls=%async_computation.3 | async-start | bytes 16384 | tf_op jit(solution)/shard_map/all_to_all | solution.py:136
  170.6 12.5 %all-to-all-start.1 = ((f32[8,2,1024]{2,1,0:T(2,128)}), f32[8,2,1024]{2,1,0:T(2,128)S(1)}, u32[]{:S(2)}, u32[]{:S(2)}) async-start(f32[8,2,1024]{2,1,0:T(2,128)} %broadcast_select_fusion), calls=%async_computation.1 | async-start | bytes 131072 | tf_op jit(solution)/shard_map/all_to_all | solution.py:135
where the time goes:
time: 185 us; the launch traced here: 184 us
  local copies, waits for them, and re-layouts  75.2 us (41%)
  other arithmetic  42.9 us (23%)
  starting transfers between devices  33.5 us (18%)
  waiting for transfers between devices  27.1 us (15%)
  loops' own time  4.01 us (2%)
    unnamed x16, local copies, waits for them, and re-layouts  21.3 us
    all_to_all x1, waiting for transfers between devices, per_device(): lax.all_to_all(intensity, 'chan', split_axis=2, concat_axis=0, tiled=True)  20.5 us
    dynamic_update_slice x2, other arithmetic, smooth_tiles(): stacked = lax.map(smooth_block, jnp.arange(chan_blocks, dtype=jnp.int32))  10.8 us
    all_to_all x2, local copies, waits for them, and re-layouts, per_device(): lax.all_to_all(intensity, 'chan', split_axis=2, concat_axis=0, tiled=True)  8.72 us
    add x2, other arithmetic, smooth_block(): sum((weights[offset] * hanning[:, offset:offset + rows_inner, :] for offs...  7.64 us
    concatenate x1, local copies, waits for them, and re-layouts, with_halo(): block = jnp.concatenate([low, block, high], axis=dim)  7.57 us
    slice x3, local copies, waits for them, and re-layouts, with_halo(): lax.slice_in_dim(block, block.shape[dim] - width, None, axis=dim)  6.64 us
    all_to_all x1, starting transfers between devices, per_device(): lax.all_to_all(spectra_slots, 'tile', split_axis=0, concat_axis=0, tiled=...  6.62 us
  transfers between devices with their start and end apart: 8, of which 3 were waited for; matrix products, arithmetic and copies ran while one was open for 31% of the time, Pallas kernels for 0%

commit v1 on v0

--- a/solution.py
+++ b/solution.py
@@ -70,7 +70,16 @@
 
 
 def per_device(intensity, block_pick, owner_tile, source_index, mask_low, mask_high):
-    regrouped = lax.all_to_all(intensity, "chan", split_axis=2, concat_axis=0, tiled=True)
+
+    def drive_the_record(vector, mesh_ax):
+        return jnp.concatenate(
+            lax.all_to_all(
+                jnp.stack(jnp.split(vector, lax.psum(1, mesh_ax), axis=2)), mesh_ax, 0, 0
+            ),
+            axis=0,
+        )
+
+    regrouped = drive_the_record(intensity, "chan")
     framed = with_halo(regrouped, (("chan", 2), ("tile", 1)), RADIUS)
     tile_cube = smooth_tiles(framed)
     chan_total, rows_inner, cols_inner = tile_cube.shape

time: 185 us -> 161 us (0.87)
  local copies, waits for them, and re-layouts: 75.2 us -> 49.7 us
    unnamed x16 -> x13, local copies, waits for them, and re-layouts: 21.3 us -> 2.58 us
    all_to_all x2 -> x0, local copies, waits for them, and re-layouts: 8.72 us -> none  [per_device(): lax.all_to_all(intensity, 'chan', split_axis=2, concat_axis=0, tiled=True)]
    another operation x0 -> x1, local copies, waits for them, and re-layouts: none -> 1.97 us  [drive_the_record(): jnp.stack(jnp.split(vector, lax.psum(1, mesh_ax), axis=2))]
  transfers between devices with their start and end apart: 8 -> 8, of which waited for: 3 -> 3; matrix products, arithmetic and copies ran while one was open for 31% -> 27% of each run, Pallas kernels for 0% -> 0%
where the time goes in v1:
time: 161 us; the launch traced here: 159 us
  local copies, waits for them, and re-layouts  49.7 us (31%)
  other arithmetic  44.3 us (28%)
  starting transfers between devices  32.4 us (20%)
  waiting for transfers between devices  28 us (17%)
  loops' own time  4.01 us (2%)
    all_to_all x1, waiting for transfers between devices, drive_the_record(): lax.all_to_all(jnp.stack(jnp.split(vector, lax.psum(1, mesh_ax), axis=2))...  20.5 us
    dynamic_update_slice x2, other arithmetic, smooth_tiles(): stacked = lax.map(smooth_block, jnp.arange(chan_blocks, dtype=jnp.int32))  10.7 us
    concatenate x1, local copies, waits for them, and re-layouts, with_halo(): block = jnp.concatenate([low, block, high], axis=dim)  7.58 us
    add x2, other arithmetic, smooth_block(): sum((weights[offset] * hanning[:, offset:offset + rows_inner, :] for offs...  7.52 us
    slice x3, local copies, waits for them, and re-layouts, with_halo(): lax.slice_in_dim(block, block.shape[dim] - width, None, axis=dim)  6.63 us
    all_to_all x1, starting transfers between devices, per_device(): lax.all_to_all(spectra_slots, 'tile', split_axis=0, concat_axis=0, tiled=...  6.62 us
    all_to_all x1, starting transfers between devices, per_device(): lax.all_to_all(tags, 'tile', split_axis=0, concat_axis=0, tiled=True)  6.6 us
    concatenate x2, other arithmetic, with_halo(): block = jnp.concatenate([low, block, high], axis=dim)  6.21 us
  transfers between devices with their start and end apart: 8, of which 3 were waited for; matrix products, arithmetic and copies ran while one was open for 27% of the time, Pallas kernels for 0%

profile of v1, /device:TPU:4, one launch (start us, length us, event | category | flops | bytes accessed | tf_op | source)
XLA Modules:
  0.0 159.4 jit_solution(3114971557453487257)
XLA Ops:
  0.6 2.0 %slice_bitcast_fusion.3 = (bf16[1,64,32,128]{3,2,1,0:T(8,128)(2,1)S(1)}, bf16[1,64,32,128]{3,2,1,0:T(8,128)(2,1)S(1)}, bf16[1,64,32,128]{3,2,1,0:T(8,128)(2,1)S(1)}, bf16[1,64,32,128]{3,2,1,0:T(8,128)(2,1)S(1)}) fusion(bf16[64,32,512]{2,1,0:T(8,128)(2,1)} %param.8), kind=kLoop, calls=%fused_computation.45 | loop fusion | bytes 4194304 | tf_op jit(solution)/shard_map/stack | solution.py:77
  2.6 1.6 pad_maximum_fusion.2
  4.2 3.7 %all-to-all-start = ((bf16[4,64,32,128]{3,2,1,0:T(8,128)(2,1)}), bf16[4,64,32,128]{3,2,1,0:T(8,128)(2,1)S(1)}, u32[]{:S(2)}, u32[]{:S(2)}) async-start(bf16[4,64,32,128]{3,2,1,0:T(8,128)(2,1)} %pad_maximum_fusion.2), calls=%async_computation | async-start | bytes 4194304 | tf_op jit(solution)/shard_map/all_to_all | solution.py:76
  8.3 0.7 gather_fusion
  8.9 0.7 gather_fusion.2
  9.8 0.7 gather_fusion.3
  11.2 20.5 %all-to-all-done = bf16[4,64,32,128]{3,2,1,0:T(8,128)(2,1)S(1)} async-done(((bf16[4,64,32,128]{3,2,1,0:T(8,128)(2,1)}), bf16[4,64,32,128]{3,2,1,0:T(8,128)(2,1)S(1)}, u32[]{:S(2)}, u32[]{:S(2)}) %all-to-all-start) | async-done | bytes 2097184 | tf_op jit(solution)/shard_map/all_to_all | solution.py:76
  31.7 6.6 %all-to-all-start.2 = ((s32[8,2,2]{1,2,0:T(2,128)}), s32[8,2,2]{1,2,0:T(2,128)S(1)}, u32[]{:S(2)}, u32[]{:S(2)}) async-start(s32[8,2,2]{1,2,0:T(2,128)} %copy.52), calls=%async_computation.2 | async-start | bytes 16384 | tf_op jit(solution)/shard_map/all_to_all | solution.py:146
  38.3 3.0 %fusion.34 = (bf16[256,32,2]{2,1,0:T(8,128)(2,1)}, bf16[256,32,2]{2,1,0:T(8,128)(2,1)}) fusion(bf16[256,32,128]{2,1,0:T(8,128)(2,1)S(1)} %bitcast.85), kind=kLoop, calls=%fused_computation.90 | loop fusion | bytes 131072 | tf_op jit(solution)/shard_map/slice | solution.py:20
  41.2 3.3 %copy.44 = bf16[256,32,2]{0,1,2:T(8,128)(2,1)S(1)} copy(bf16[256,32,2]{2,1,0:T(8,128)(2,1)} %get-tuple-element.92) | data formatting | bytes 65536 | tf_op jit(solution)/shard_map/slice | solution.py:20
  44.5 1.9 %collective-permute-start = (bf16[256,32,2]{0,1,2:T(8,128)(2,1)S(1)}, bf16[256,32,2]{0,1,2:T(8,128)(2,1)S(1)}, u32[]{:S(2)}, u32[]{:S(2)}) collective-permute-start(bf16[256,32,2]{0,1,2:T(8,128)(2,1)S(1)} %copy.44), channel_id=1, source_target_pairs={{0,8},{8,16},{16,24},{1,9},{9,17},{17,25},{2,10},{10,18},{18,26},{... | collective-permute-start | bytes 98312 | tf_op jit(solution)/shard_map/ppermute | solution.py:19
  46.4 3.3 %copy.45 = bf16[256,32,2]{0,1,2:T(8,128)(2,1)S(1)} copy(bf16[256,32,2]{2,1,0:T(8,128)(2,1)} %get-tuple-element.93) | data formatting | bytes 65536 | tf_op jit(solution)/shard_map/slice | solution.py:22
  49.7 3.6 %collective-permute-start.1 = (bf16[256,32,2]{0,1,2:T(8,128)(2,1)S(1)}, bf16[256,32,2]{0,1,2:T(8,128)(2,1)S(1)}, u32[]{:S(2)}, u32[]{:S(2)}) collective-permute-start(bf16[256,32,2]{0,1,2:T(8,128)(2,1)S(1)} %copy.45), channel_id=1, source_target_pairs={{8,0},{16,8},{24,16},{9,1},{17,9},{25,17},{10,2},{18,10},{26,18},{... | collective-permute-start | bytes 98312 | tf_op jit(solution)/shard_map/ppermute | solution.py:22
  54.0 4.2 %copy.46 = bf16[256,32,2]{2,1,0:T(8,128)(2,1)} copy(bf16[256,32,2]{0,1,2:T(8,128)(2,1)S(1)} %collective-permute-done) | data formatting | bytes 65536 | tf_op jit(solution)/shard_map/ppermute | solution.py:19
  58.2 4.2 %copy.47 = bf16[256,32,2]{2,1,0:T(8,128)(2,1)} copy(bf16[256,32,2]{0,1,2:T(8,128)(2,1)S(1)} %collective-permute-done.1) | data formatting | bytes 65536 | tf_op jit(solution)/shard_map/ppermute | solution.py:22
  62.4 4.3 %pad_maximum_fusion = bf16[256,32,132]{2,1,0:T(8,128)(2,1)S(1)} fusion(bf16[256,32,2]{2,1,0:T(8,128)(2,1)} %copy.47, bf16[256,32,128]{2,1,0:T(8,128)(2,1)S(1)} %bitcast.86, bf16[256,32,2]{2,1,0:T(8,128)(2,1)} %copy.46), kind=kLoop, calls=%fused_computation.33 | loop fusion | flops 6488064 | bytes 4325376 | tf_op jit(solution)/shard_map/concatenate | solution.py:23
  66.7 1.9 %copy-done.5 = bf16[256,32,132]{2,1,0:T(8,128)(2,1)} copy-done((bf16[256,32,132]{2,1,0:T(8,128)(2,1)}, bf16[256,32,132]{2,1,0:T(8,128)(2,1)S(1)}, u32[]{:S(2)}) %copy-start.5) | copy-done | bytes 2162712
  69.0 3.9 %collective-permute-start.2 = (bf16[256,2,132]{2,1,0:T(2,128)(2,1)S(1)}, bf16[256,2,132]{2,1,0:T(2,128)(2,1)S(1)}, u32[]{:S(2)}, u32[]{:S(2)}) collective-permute-start(bf16[256,2,132]{2,1,0:T(2,128)(2,1)S(1)} %get-tuple-element.90), channel_id=1, source_target_pairs={{0,1},{1,2},{2,3},{3,4},{4,5},{5,6},{6,7},{8,9},{9,10},{10,11},{11... | collective-permute-start | bytes 405512 | tf_op jit(solution)/shard_map/ppermute | solution.py:19
  72.9 1.3 collective-permute-start.3
  74.2 0.7 broadcast_divide_fusion
  76.0 0.8 scatter_custom_fusion.1
  77.2 7.6 %copy.49 = bf16[256,32,132]{0,2,1:T(8,128)(2,1)} copy(bf16[256,32,132]{2,1,0:T(8,128)(2,1)} %copy-done.5) | data formatting | bytes 4325376 | tf_op jit(solution)/shard_map/concatenate | solution.py:23
  85.2 2.0 %pad_maximum_fusion.1 = bf16[256,36,132]{0,2,1:T(8,128)(2,1)S(1)} fusion(bf16[256,2,132]{0,2,1:T(8,128)(2,1)S(1)} %copy.50, bf16[256,32,132]{0,2,1:T(8,128)(2,1)} %copy.49, bf16[256,2,132]{0,2,1:T(8,128)(2,1)S(1)} %copy.48), kind=kLoop, calls=%fused_computation.40 | loop fusion | flops 2433024 | bytes 4866048 | tf_op jit(solution)/shard_map/concatenate | solution.py:23
  87.1 38.6 %while.12 = (s32[]{:T(128)}, bf16[2,128,32,128]{1,3,2,0:T(8,128)(2,1)}, f32[5]{0:T(128)S(1)}, s32[2]{0:T(128)S(1)}, bf16[256,36,132]{0,2,1:T(8,128)(2,1)S(1)}, /...) while((s32[]{:T(128)}, ...), condition=%wide.region_6.7_spmd, body=%wide.region_5.6_spmd.sunk | while | flops 14994001 | bytes 46544248 | solution.py:68
  89.7 3.0 %convert_multiply_fusion.3 = (f32[1,36,132]{0,2,1:T(8,128)}, f32[1,36,132]{0,2,1:T(8,128)}) fusion(f32[]{:T(128)} %bitcast.76, bf16[256,36,132]{0,2,1:T(8,128)(2,1)S(1)} %get-tuple-element.179, s32[]{:T(128)S(6)} %select_n.117, f32[]{:T(128)} %bitcast.77, s32[]{:T(128)S(6)} %max.7), kind=kLoop, calls=%fused_computation.10.clone.1 | loop fusion | flops 19008 | bytes 57040 | tf_op jit(solution)/shard_map/while/body/eval_jaxpr/mul | solution.py:50
  92.9 0.8 fusion.40
  93.7 0.9 copy-done.3
  94.6 0.8 copy-done.4
  95.3 1.4 fusion.41
  96.7 0.7 fusion.42
  97.4 3.8 %fusion.43 = f32[128,32,132]{0,2,1:T(8,128)S(1)} fusion(f32[128,36,132]{0,2,1:T(8,128)S(1)} %fusion.41, f32[]{:T(128)} %bitcast.78, f32[]{:T(128)} %bitcast.79, f32[]{:T(128)} %bitcast.80, f32[]{:T(128)} %bitcast.81, f32[]{:T(128)} %bitcast.82), kind=kLoop, calls=%fused_computation.13.clone.1 | loop fusion | flops 4866048 | bytes 12976148 | tf_op jit(solution)/shard_map/while/body/eval_jaxpr/add | solution.py:54
  101.1 5.3 %bitcast_dynamic-update-slice_fusion.2 = bf16[2,128,32,128]{1,3,2,0:T(8,128)(2,1)} fusion(bf16[2,128,32,128]{1,3,2,0:T(8,128)(2,1)} %get-tuple-element.162, s32[]{:T(128)} %get-tuple-element.161, f32[128,32,132]{0,2,1:T(8,128)S(1)} %fusion.43, f32[]{:T(128)} %bitcast.78, f32[]{:T(128)} %bitcast.79, f32[]{:T(128)} %bitcast.80, f32[]{:T(128)} %bitcast.81, ...), kind=kLoop, calls=%fused_computation.32.clone.1 | loop fusion | flops 5242880 | bytes 11537408 | tf_op jit(solution)/shard_map/while/body/jit(dynamic_update_index_in_dim)/dynamic_update_slice | solution.py:68
  109.0 3.0 %convert_multiply_fusion.3 = (f32[1,36,132]{0,2,1:T(8,128)}, f32[1,36,132]{0,2,1:T(8,128)}) fusion(f32[]{:T(128)} %bitcast.76, bf16[256,36,132]{0,2,1:T(8,128)(2,1)S(1)} %get-tuple-element.179, s32[]{:T(128)S(6)} %select_n.117, f32[]{:T(128)} %bitcast.77, s32[]{:T(128)S(6)} %max.7), kind=kLoop, calls=%fused_computation.10.clone.1 | loop fusion | flops 19008 | bytes 57040 | tf_op jit(solution)/shard_map/while/body/eval_jaxpr/mul | solution.py:50
  112.2 0.8 fusion.40
  113.0 0.9 copy-done.3
  113.9 0.8 copy-done.4
  114.6 1.4 fusion.41
  116.0 0.7 fusion.42
  116.7 3.8 %fusion.43 = f32[128,32,132]{0,2,1:T(8,128)S(1)} fusion(f32[128,36,132]{0,2,1:T(8,128)S(1)} %fusion.41, f32[]{:T(128)} %bitcast.78, f32[]{:T(128)} %bitcast.79, f32[]{:T(128)} %bitcast.80, f32[]{:T(128)} %bitcast.81, f32[]{:T(128)} %bitcast.82), kind=kLoop, calls=%fused_computation.13.clone.1 | loop fusion | flops 4866048 | bytes 12976148 | tf_op jit(solution)/shard_map/while/body/eval_jaxpr/add | solution.py:54
  120.4 5.3 %bitcast_dynamic-update-slice_fusion.2 = bf16[2,128,32,128]{1,3,2,0:T(8,128)(2,1)} fusion(bf16[2,128,32,128]{1,3,2,0:T(8,128)(2,1)} %get-tuple-element.162, s32[]{:T(128)} %get-tuple-element.161, f32[128,32,132]{0,2,1:T(8,128)S(1)} %fusion.43, f32[]{:T(128)} %bitcast.78, f32[]{:T(128)} %bitcast.79, f32[]{:T(128)} %bitcast.80, f32[]{:T(128)} %bitcast.81, ...), kind=kLoop, calls=%fused_computation.32.clone.1 | loop fusion | flops 5242880 | bytes 11537408 | tf_op jit(solution)/shard_map/while/body/jit(dynamic_update_index_in_dim)/dynamic_update_slice | solution.py:68
  125.8 6.1 %fusion.11 = (f32[2,128,128]{1,2,0:T(8,128)S(1)}, f32[2,32,128]{2,1,0:T(8,128)S(1)}) fusion(bf16[2,128,32,128]{1,3,2,0:T(8,128)(2,1)} %get-tuple-element.68, s32[2,32,128]{2,1,0:T(8,128)S(1)} %lt.89, s32[2,32,128]{2,1,0:T(8,128)S(1)} %le.17), kind=kLoop, calls=%fused_computation.35 | loop fusion | flops 7299072 | bytes 2326528 | tf_op jit(solution)/shard_map/reduce_sum | solution.py:127
  133.4 0.7 broadcast_select_fusion.1
  134.0 6.6 %all-to-all-start.3 = ((f32[8,2,128]{2,1,0:T(2,128)}), f32[8,2,128]{2,1,0:T(2,128)S(1)}, u32[]{:S(2)}, u32[]{:S(2)}) async-start(f32[8,2,128]{2,1,0:T(2,128)} %broadcast_select_fusion.1), calls=%async_computation.3 | async-start | bytes 16384 | tf_op jit(solution)/shard_map/all_to_all | solution.py:145
  140.6 0.7 broadcast_select_fusion
  141.4 4.5 %copy.55 = bf16[2,128,32,128]{3,2,1,0:T(8,128)(2,1)} copy(bf16[2,128,32,128]{1,3,2,0:T(8,128)(2,1)} %get-tuple-element.68) | data formatting | bytes 4194304 | tf_op jit(solution)/shard_map/while | solution.py:68
  145.9 1.3 all-to-all-done.3
  147.2 4.7 %all-to-all-start.1 = ((f32[8,2,1024]{2,1,0:T(2,128)}), f32[8,2,1024]{2,1,0:T(2,128)S(1)}, u32[]{:S(2)}, u32[]{:S(2)}) async-start(f32[8,2,1024]{2,1,0:T(2,128)} %broadcast_select_fusion), calls=%async_computation.1 | async-start | bytes 131072 | tf_op jit(solution)/shard_map/all_to_all | solution.py:144
  152.6 6.2 %all-to-all-done.1 = f32[8,2,1024]{2,1,0:T(2,128)S(1)} async-done(((f32[8,2,1024]{2,1,0:T(2,128)}), f32[8,2,1024]{2,1,0:T(2,128)S(1)}, u32[]{:S(2)}, u32[]{:S(2)}) %all-to-all-start.1) | async-done | bytes 65568 | tf_op jit(solution)/shard_map/all_to_all | solution.py:144
  (65 shorter events, 8.4 us)
Async XLA Ops:
  0.6 74.4 %copy-start = (s32[1,1,4,1024]{3,2,1,0:T(4,128)S(1)}, s32[1,1,4,1024]{3,2,1,0:T(4,128)}, u32[]{:S(2)}) copy-start(s32[1,1,4,1024]{3,2,1,0:T(4,128)} %param.12) | copy-start | bytes 49156
  4.2 3.7 %copy-start.7 = (s32[1,1,4]{2,1,0:T(1,128)S(1)}, s32[1,1,4]{2,1,0:T(1,128)}, u32[]{:S(2)}) copy-start(s32[1,1,4]{2,1,0:T(1,128)} %param.10) | copy-start | bytes 52
  4.2 4.0 %copy-start.2 = (s32[1,1,4]{2,1,0:T(1,128)S(1)}, s32[1,1,4]{2,1,0:T(1,128)}, u32[]{:S(2)}) copy-start(s32[1,1,4]{2,1,0:T(1,128)} %param.9) | copy-start | bytes 52
  4.2 4.7 %copy-start.1 = (s32[1,1,4]{2,1,0:T(1,128)S(1)}, s32[1,1,4]{2,1,0:T(1,128)}, u32[]{:S(2)}) copy-start(s32[1,1,4]{2,1,0:T(1,128)} %param.11) | copy-start | bytes 52
  4.2 27.5 %all-to-all-start = ((bf16[4,64,32,128]{3,2,1,0:T(8,128)(2,1)}), bf16[4,64,32,128]{3,2,1,0:T(8,128)(2,1)S(1)}, u32[]{:S(2)}, u32[]{:S(2)}) async-start(bf16[4,64,32,128]{3,2,1,0:T(8,128)(2,1)} %pad_maximum_fusion.2), calls=%async_computation | async-start | bytes 4194304 | tf_op jit(solution)/shard_map/all_to_all | solution.py:76
  31.7 45.4 %all-to-all-start.2 = ((s32[8,2,2]{1,2,0:T(2,128)}), s32[8,2,2]{1,2,0:T(2,128)S(1)}, u32[]{:S(2)}, u32[]{:S(2)}) async-start(s32[8,2,2]{1,2,0:T(2,128)} %copy.52), calls=%async_computation.2 | async-start | bytes 16384 | tf_op jit(solution)/shard_map/all_to_all | solution.py:146
  44.5 9.5 %collective-permute-start = (bf16[256,32,2]{0,1,2:T(8,128)(2,1)S(1)}, bf16[256,32,2]{0,1,2:T(8,128)(2,1)S(1)}, u32[]{:S(2)}, u32[]{:S(2)}) collective-permute-start(bf16[256,32,2]{0,1,2:T(8,128)(2,1)S(1)} %copy.44), channel_id=1, source_target_pairs={{0,8},{8,16},{16,24},{1,9},{9,17},{17,25},{2,10},{10,18},{18,26},{... | collective-permute-start | bytes 98312 | tf_op jit(solution)/shard_map/ppermute | solution.py:19
  49.7 8.5 %collective-permute-start.1 = (bf16[256,32,2]{0,1,2:T(8,128)(2,1)S(1)}, bf16[256,32,2]{0,1,2:T(8,128)(2,1)S(1)}, u32[]{:S(2)}, u32[]{:S(2)}) collective-permute-start(bf16[256,32,2]{0,1,2:T(8,128)(2,1)S(1)} %copy.45), channel_id=1, source_target_pairs={{8,0},{16,8},{24,16},{9,1},{17,9},{25,17},{10,2},{18,10},{26,18},{... | collective-permute-start | bytes 98312 | tf_op jit(solution)/shard_map/ppermute | solution.py:22
  62.4 13.6 %copy-start.6 = (s32[1,1,4,1024]{3,2,1,0:T(4,128)S(1)}, s32[1,1,4,1024]{3,2,1,0:T(4,128)}, u32[]{:S(2)}) copy-start(s32[1,1,4,1024]{3,2,1,0:T(4,128)} %param.13) | copy-start | bytes 49156
  66.6 1.9 %copy-start.5 = (bf16[256,32,132]{2,1,0:T(8,128)(2,1)}, bf16[256,32,132]{2,1,0:T(8,128)(2,1)S(1)}, u32[]{:S(2)}) copy-start(bf16[256,32,132]{2,1,0:T(8,128)(2,1)S(1)} %pad_maximum_fusion) | copy-start | bytes 6488068
  69.0 15.8 %collective-permute-start.2 = (bf16[256,2,132]{2,1,0:T(2,128)(2,1)S(1)}, bf16[256,2,132]{2,1,0:T(2,128)(2,1)S(1)}, u32[]{:S(2)}, u32[]{:S(2)}) collective-permute-start(bf16[256,2,132]{2,1,0:T(2,128)(2,1)S(1)} %get-tuple-element.90), channel_id=1, source_target_pairs={{0,1},{1,2},{2,3},{3,4},{4,5},{5,6},{6,7},{8,9},{9,10},{10,11},{11... | collective-permute-start | bytes 405512 | tf_op jit(solution)/shard_map/ppermute | solution.py:19
  72.9 12.0 %collective-permute-start.3 = (bf16[256,2,132]{2,1,0:T(2,128)(2,1)S(1)}, bf16[256,2,132]{2,1,0:T(2,128)(2,1)S(1)}, u32[]{:S(2)}, u32[]{:S(2)}) collective-permute-start(bf16[256,2,132]{2,1,0:T(2,128)(2,1)S(1)} %get-tuple-element.91), channel_id=1, source_target_pairs={{1,0},{2,1},{3,2},{4,3},{5,4},{6,5},{7,6},{9,8},{10,9},{11,10},{12... | collective-permute-start | bytes 405512 | tf_op jit(solution)/shard_map/ppermute | solution.py:22
  92.9 1.7 %copy-start.3 = (f32[1,36,132]{0,2,1:T(8,128)S(1)}, f32[1,36,132]{0,2,1:T(8,128)}, u32[]{:S(2)}) copy-start(f32[1,36,132]{0,2,1:T(8,128)} %get-tuple-element.140) | copy-start | bytes 57028 | tf_op jit(solution)/shard_map/while
  92.9 2.5 %copy-start.4 = (f32[1,36,132]{0,2,1:T(8,128)S(1)}, f32[1,36,132]{0,2,1:T(8,128)}, u32[]{:S(2)}) copy-start(f32[1,36,132]{0,2,1:T(8,128)} %get-tuple-element.139) | copy-start | bytes 57028 | tf_op jit(solution)/shard_map/while
  112.2 1.7 %copy-start.3 = (f32[1,36,132]{0,2,1:T(8,128)S(1)}, f32[1,36,132]{0,2,1:T(8,128)}, u32[]{:S(2)}) copy-start(f32[1,36,132]{0,2,1:T(8,128)} %get-tuple-element.140) | copy-start | bytes 57028 | tf_op jit(solution)/shard_map/while
  112.2 2.5 %copy-start.4 = (f32[1,36,132]{0,2,1:T(8,128)S(1)}, f32[1,36,132]{0,2,1:T(8,128)}, u32[]{:S(2)}) copy-start(f32[1,36,132]{0,2,1:T(8,128)} %get-tuple-element.139) | copy-start | bytes 57028 | tf_op jit(solution)/shard_map/while
  134.0 13.1 %all-to-all-start.3 = ((f32[8,2,128]{2,1,0:T(2,128)}), f32[8,2,128]{2,1,0:T(2,128)S(1)}, u32[]{:S(2)}, u32[]{:S(2)}) async-start(f32[8,2,128]{2,1,0:T(2,128)} %broadcast_select_fusion.1), calls=%async_computation.3 | async-start | bytes 16384 | tf_op jit(solution)/shard_map/all_to_all | solution.py:145
  147.2 11.6 %all-to-all-start.1 = ((f32[8,2,1024]{2,1,0:T(2,128)}), f32[8,2,1024]{2,1,0:T(2,128)S(1)}, u32[]{:S(2)}, u32[]{:S(2)}) async-start(f32[8,2,1024]{2,1,0:T(2,128)} %broadcast_select_fusion), calls=%async_computation.1 | async-start | bytes 131072 | tf_op jit(solution)/shard_map/all_to_all | solution.py:144
